TPU v7x, 32 devices: a whole 2x2x4 slice. The times are simulated.
32 devices in a mesh: ctx: 4 (over x, core), head: 8 (over z, y).
Axes of the slice: x: 2, y: 2, z: 4, core: 2. Of those that a mesh axis runs over, the one named last changes fastest.
Arguments:
- queries: bfloat16 [2048, 16, 128], P('ctx', 'head'), may hold values from -42 to 42
- cached_keys: bfloat16 [1, 16384, 128], P(None, 'ctx'), may hold values from -5 to 5
- cached_values: bfloat16 [1, 16384, 128], P(None, 'ctx'), may hold values from -6 to 6
- grad_out: bfloat16 [2048, 16, 128], P('ctx', 'head'), may hold values from -96 to 96
- chosen: int32 [1, 8, 16], P(None, 'ctx'), may hold values from 0 to 255, as said below
- counts: int32 [1, 8], P(None, 'ctx'), may hold values from 8 to 16, as said below
Outputs:
- grad_query: bfloat16 [2048, 16, 128], P('ctx', 'head')
- grad_keys: bfloat16 [1, 16384, 128], P(None, ('ctx', 'head'))
- grad_values: bfloat16 [1, 16384, 128], P(None, ('ctx', 'head'))
Inputs may be any that keep to these rules, and one draw needn't show every extreme that they name: For t < counts[g, b] the entries chosen[g, b, t] are distinct; entries at t >= counts[g, b] are padding. For each group and each run of 2 query blocks starting at a multiple of 2, at most 8 live entries fall in one range of 64 blocks starting at a multiple of 64, and in every group one range receives exactly 8 from every such run. `counts`: in every group some query block has 16 live entries.
All inputs are finite; a program needn't handle non-finite values.
Results may differ from a plain program's by a relative error of at most 0.02.
Values may be sent and summed in bfloat16 or wider, within the bound.
A program may use at most 64 MiB of HBM per device.

v0:
```python
import jax
import jax.numpy as jnp
from jax import lax
from jax.sharding import PartitionSpec as P

DH = 128
HPG = 16
HEAD_DEV = 2
KBS = 64
TOPB = 16
QBS = 256
QB_DEV = 2
KV_DEV = 4096
BLK_OWN = 64
CAP = 8


def body(queries, cached_keys, cached_values, grad_out, chosen, counts):
    inv_root = DH ** (-0.5)
    owners = lax.axis_size("ctx")
    head_count = lax.axis_size("head")
    per_group = HPG // HEAD_DEV
    my_group = lax.axis_index("head") // per_group
    picked = lax.dynamic_index_in_dim(chosen, my_group, 0, keepdims=False)
    live_count = lax.dynamic_index_in_dim(counts, my_group, 0, keepdims=False)
    slot_live = (jnp.arange(TOPB)[None, :] < live_count[:, None]).reshape(-1)
    flat_pick = picked.reshape(-1)
    owner_index = flat_pick // BLK_OWN
    local_index = flat_pick % BLK_OWN
    member = ((owner_index[:, None] == jnp.arange(owners)[None, :]) & slot_live[:, None]).astype(
        jnp.int32
    )
    earlier = jnp.cumsum(member, axis=0) - member
    rank_index = jnp.sum(earlier * member, axis=1)
    position = owner_index * CAP + rank_index
    target = jnp.where(slot_live, position, owners * CAP)
    requests = (
        jnp.zeros((owners * CAP,), jnp.int32)
        .at[target]
        .set(local_index, mode="drop")
        .reshape(owners, CAP)
    )
    own_keys = lax.dynamic_index_in_dim(cached_keys, my_group, 0, keepdims=False).reshape(
        BLK_OWN, KBS * DH
    )
    own_values = lax.dynamic_index_in_dim(cached_values, my_group, 0, keepdims=False).reshape(
        BLK_OWN, KBS * DH
    )
    asked_rows = lax.all_to_all(requests, "ctx", split_axis=0, concat_axis=0, tiled=True)
    key_rows = jnp.take(own_keys, asked_rows, axis=0)
    value_rows = jnp.take(own_values, asked_rows, axis=0)
    key_back = lax.all_to_all(key_rows, "ctx", split_axis=0, concat_axis=0, tiled=True)
    value_back = lax.all_to_all(value_rows, "ctx", split_axis=0, concat_axis=0, tiled=True)
    gather_at = jnp.where(slot_live, position, 0)
    selected_keys = jnp.take(key_back.reshape(owners * CAP, KBS * DH), gather_at, axis=0).reshape(
        QB_DEV, TOPB * KBS, DH
    )
    selected_values = jnp.take(
        value_back.reshape(owners * CAP, KBS * DH), gather_at, axis=0
    ).reshape(QB_DEV, TOPB * KBS, DH)
    key_live = jnp.repeat(slot_live.reshape(QB_DEV, TOPB), KBS, axis=1)
    live_mask = key_live[:, None, None, :]
    query_block_rows = queries.reshape(QB_DEV, QBS, HEAD_DEV, DH)
    block_gradients = grad_out.reshape(QB_DEV, QBS, HEAD_DEV, DH)
    logit_scores = (
        jnp.einsum(
            "eryj,ezj->eyrz", query_block_rows, selected_keys, preferred_element_type=jnp.float32
        )
        * inv_root
    )
    row_peak = jnp.max(jnp.where(live_mask, logit_scores, -jnp.inf), axis=-1, keepdims=True)
    weights_raw = jnp.where(live_mask, jnp.exp(logit_scores - row_peak), 0.0)
    weights = weights_raw / jnp.sum(weights_raw, axis=-1, keepdims=True)
    weight_halves = weights.astype(jnp.bfloat16)
    attn_out = jnp.einsum(
        "npsr,nry->nspy", weight_halves, selected_values, preferred_element_type=jnp.float32
    ).astype(jnp.bfloat16)
    attn_wide = lax.optimization_barrier(attn_out).astype(jnp.float32)
    row_dot = jnp.sum(block_gradients.astype(jnp.float32) * attn_wide, axis=-1)
    row_dot = jnp.transpose(row_dot, (0, 2, 1))[:, :, :, None]
    grad_weights = jnp.einsum(
        "eryj,ezj->eyrz", block_gradients, selected_values, preferred_element_type=jnp.float32
    )
    score_gradients = (weights * (grad_weights - row_dot) * inv_root).astype(jnp.bfloat16)
    grad_query = jnp.einsum(
        "npsr,nry->nspy", score_gradients, selected_keys, preferred_element_type=jnp.float32
    )
    grad_query = grad_query.astype(jnp.bfloat16).reshape(QB_DEV * QBS, HEAD_DEV, DH)
    slot_dk = jnp.einsum(
        "lxsi,lsxr->lir", score_gradients, query_block_rows, preferred_element_type=jnp.float32
    ).reshape(QB_DEV * TOPB, KBS * DH)
    slot_dv = jnp.einsum(
        "lxsi,lsxr->lir", weight_halves, block_gradients, preferred_element_type=jnp.float32
    ).reshape(QB_DEV * TOPB, KBS * DH)
    home_dk = (
        jnp.zeros((owners * CAP, KBS * DH), jnp.float32)
        .at[target]
        .set(slot_dk, mode="drop")
        .reshape(owners, CAP, KBS * DH)
    )
    home_dv = (
        jnp.zeros((owners * CAP, KBS * DH), jnp.float32)
        .at[target]
        .set(slot_dv, mode="drop")
        .reshape(owners, CAP, KBS * DH)
    )
    block_match = (asked_rows.reshape(-1)[None, :] == jnp.arange(BLK_OWN)[:, None]).astype(
        jnp.float32
    )
    groups = head_count // per_group
    piece_rows = KV_DEV // head_count
    recv_dk, recv_dv = (
        lax.all_to_all(
            home_dk.astype(jnp.bfloat16), "ctx", split_axis=0, concat_axis=0, tiled=True
        ).astype(home_dk.dtype),
        lax.all_to_all(
            home_dv.astype(jnp.bfloat16), "ctx", split_axis=0, concat_axis=0, tiled=True
        ).astype(home_dv.dtype),
    )
    total_dk = jnp.dot(
        block_match,
        recv_dk.reshape(owners * CAP, KBS * DH),
        precision=lax.Precision.HIGHEST,
        preferred_element_type=jnp.float32,
    ).reshape(KV_DEV, DH)
    total_dv = jnp.dot(
        block_match,
        recv_dv.reshape(owners * CAP, KBS * DH),
        precision=lax.Precision.HIGHEST,
        preferred_element_type=jnp.float32,
    ).reshape(KV_DEV, DH)
    sent_dk = total_dk.reshape(head_count, piece_rows, DH)
    sent_dv = total_dv.reshape(head_count, piece_rows, DH)
    got_dk, got_dv = (
        lax.all_to_all(
            sent_dk.astype(jnp.bfloat16), "head", split_axis=0, concat_axis=0, tiled=True
        ).astype(sent_dk.dtype),
        lax.all_to_all(
            sent_dv.astype(jnp.bfloat16), "head", split_axis=0, concat_axis=0, tiled=True
        ).astype(sent_dv.dtype),
    )
    grad_keys = jnp.sum(got_dk.reshape(groups, per_group, piece_rows, DH), axis=1)
    grad_values = jnp.sum(got_dv.reshape(groups, per_group, piece_rows, DH), axis=1)
    return (grad_query, grad_keys.astype(jnp.bfloat16), grad_values.astype(jnp.bfloat16))


def solution(mesh):
    return jax.shard_map(
        body,
        mesh=mesh,
        in_specs=(
            P("ctx", "head", None),
            P(None, "ctx", None),
            P(None, "ctx", None),
            P("ctx", "head", None),
            P(None, "ctx", None),
            P(None, "ctx"),
        ),
        out_specs=(
            P("ctx", "head", None),
            P(None, ("ctx", "head"), None),
            P(None, ("ctx", "head"), None),
        ),
        check_vma=False,
    )
```

profile of v0, /device:TPU:0, one launch (start us, length us, event | category | flops | bytes accessed | tf_op | source)
XLA Modules:
  0.0 145.7 jit_solution(1213152681715831100)
XLA Ops:
  0.6 0.8 iota_compare_fusion.4
  1.4 0.1 lt.74
  1.5 0.1 lt.73
  1.6 0.8 reshape.238
  2.3 0.8 reshape.237
  3.1 0.1 fusion.30
  3.2 0.2 select_reduce_fusion
  3.5 0.7 scatter_custom_fusion
  4.1 0.7 all_to_all.26
  4.8 4.2 %all-to-all-start = ((s32[4,1,8]{2,1,0:T(1,128)}), s32[4,1,8]{2,1,0:T(1,128)S(1)}, u32[]{:S(2)}, u32[]{:S(2)}) async-start(s32[4,1,8]{2,1,0:T(1,128)} %bitcast.3), calls=%async_computation | async-start | bytes 4096 | tf_op jit(solution)/shard_map/all_to_all | solution.py:49
  9.0 1.5 %reshape.236 = bf16[64,8192]{1,0:T(8,128)(2,1)S(1)} reshape(bf16[1,4096,128]{2,1,0:T(8,128)(2,1)} %param.11) | data formatting | bytes 2097152 | tf_op jit(solution)/shard_map/reshape | solution.py:43
  10.5 1.5 %reshape.242 = bf16[64,8192]{1,0:T(8,128)(2,1)S(1)} reshape(bf16[1,4096,128]{2,1,0:T(8,128)(2,1)} %param.12) | data formatting | bytes 2097152 | tf_op jit(solution)/shard_map/reshape | solution.py:46
  12.1 0.6 all-to-all-done
  12.7 0.1 reshape.313
  12.8 0.9 gather_fusion
  13.7 0.9 gather_fusion.2
  14.6 0.9 bitcast_select_fusion.4
  15.5 11.3 %all_to_all.42 = bf16[4,8,8192]{2,1,0:T(8,128)(2,1)S(1)} all-to-all(bf16[4,8,8192]{2,1,0:T(8,128)(2,1)S(1)} %get-tuple-element.16), channel_id=1, replica_groups=mesh['ctx'=4,'head'=8] {'ctx'}, dimensions={0} | all-to-all | bytes 1048576 | tf_op jit(solution)/shard_map/all_to_all | solution.py:52
  26.8 3.5 %all-to-all-start.2 = ((bf16[4,8,8192]{2,1,0:T(8,128)(2,1)}), bf16[4,8,8192]{2,1,0:T(8,128)(2,1)S(1)}, u32[]{:S(2)}, u32[]{:S(2)}) async-start(bf16[4,8,8192]{2,1,0:T(8,128)(2,1)} %get-tuple-element.15), calls=%async_computation.2 | async-start | bytes 1048576 | tf_op jit(solution)/shard_map/all_to_all | solution.py:53
  30.3 0.1 broadcast_in_dim.58
  30.4 0.1 broadcast_in_dim.59
  30.5 0.1 copy.33
  30.7 0.9 gather_fusion.1
  31.6 7.5 %all-to-all-done.2 = bf16[4,8,8192]{2,1,0:T(8,128)(2,1)S(1)} async-done(((bf16[4,8,8192]{2,1,0:T(8,128)(2,1)}), bf16[4,8,8192]{2,1,0:T(8,128)(2,1)S(1)}, u32[]{:S(2)}, u32[]{:S(2)}) %all-to-all-start.2) | async-done | bytes 524320 | tf_op jit(solution)/shard_map/all_to_all | solution.py:53
  39.1 0.9 gather_fusion.3
  40.0 0.2 broadcast_select_fusion
  40.2 0.2 reshape.244
  40.4 1.1 reshape.326
  41.5 0.2 reshape.325
  41.7 0.7 fusion.19
  42.5 1.5 %fusion.37 = (f32[2,2,256]{2,1,0:T(2,128)S(1)}, f32[2,2,256,1024]{2,3,1,0:T(8,128)S(1)}) fusion(f32[2,1024,256,2]{2,1,3,0:T(8,128)S(1)} %fusion.19, pred[2,1024]{1,0:T(4,128)(4,1)S(1)} %broadcast_in_dim.59), kind=kOutput, calls=%fused_computation.82 | output fusion | flops 6292479 | bytes 8394752 | tf_op jit(solution)/shard_map/sub | solution.py:72
  44.0 0.3 fusion.11
  44.3 0.5 fusion.12
  44.8 1.7 %convolution_bitcast_fusion = f32[2,1024,128]{2,1,0:T(8,128)} fusion(bf16[2,2,256,1024]{2,3,1,0:T(8,128)(2,1)S(1)} %fusion.11, bf16[2,256,2,128]{1,3,2,0:T(8,128)(2,1)S(1)} %copy.33), kind=kOutput, calls=%fused_computation.25 | convolution fusion | flops 268435456 | bytes 3407872 | tf_op jit(solution)/shard_map/lxsi,lsxr->lir/dot_general | solution.py:92
  46.5 0.1 multiply_reduce_fusion
  46.6 0.8 fusion.3
  47.4 1.7 %convolution_bitcast_fusion.1 = f32[2,1024,128]{2,1,0:T(8,128)} fusion(bf16[2,2,256,1024]{2,3,1,0:T(8,128)(2,1)S(1)} %fusion.3, bf16[2,256,2,128]{3,2,1,0:T(2,128)(2,1)S(1)} %bitcast.88), kind=kOutput, calls=%fused_computation.26 | convolution fusion | flops 268435456 | bytes 3407872 | tf_op jit(solution)/shard_map/lxsi,lsxr->lir/dot_general | solution.py:89
  49.1 2.4 %reshape.295 = f32[32,8192]{1,0:T(8,128)} reshape(f32[2,1024,128]{2,1,0:T(8,128)} %convolution_bitcast_fusion.1) | data formatting | bytes 2097152 | tf_op jit(solution)/shard_map/reshape | solution.py:91
  51.5 2.9 %scatter_custom_fusion.1 = f32[32,8192]{1,0:T(8,128)} fusion(s32[32]{0:T(128)S(1)} %fusion.31, f32[32,8192]{1,0:T(8,128)} %reshape.295, f32[]{:T(128)} %constant.93.clone.1), kind=kCustom, calls=%fused_computation.44 | custom fusion | bytes 1049088 | tf_op jit(solution)/shard_map/scatter | solution.py:98
  54.4 2.1 %convert_bitcast_fusion.1 = bf16[4,8,8192]{2,1,0:T(8,128)(2,1)} fusion(f32[32,8192]{1,0:T(8,128)} %scatter_custom_fusion.1), kind=kLoop, calls=%fused_computation.41 | loop fusion | flops 262144 | bytes 1572864 | tf_op jit(solution)/shard_map/convert_element_type | solution.py:114
  56.5 3.5 %all-to-all-start.3 = ((bf16[4,8,8192]{2,1,0:T(8,128)(2,1)}), bf16[4,8,8192]{2,1,0:T(8,128)(2,1)S(1)}, u32[]{:S(2)}, u32[]{:S(2)}) async-start(bf16[4,8,8192]{2,1,0:T(8,128)(2,1)} %convert_bitcast_fusion.1), calls=%async_computation.3 | async-start | bytes 1048576 | tf_op jit(solution)/shard_map/all_to_all | solution.py:113
  59.9 2.5 %reshape.303 = f32[32,8192]{1,0:T(8,128)} reshape(f32[2,1024,128]{2,1,0:T(8,128)} %convolution_bitcast_fusion) | data formatting | bytes 2097152 | tf_op jit(solution)/shard_map/reshape | solution.py:94
  62.4 2.9 %scatter_custom_fusion.2 = f32[32,8192]{1,0:T(8,128)} fusion(s32[32]{0:T(128)S(1)} %fusion.31, f32[32,8192]{1,0:T(8,128)} %reshape.303, f32[]{:T(128)} %constant.93.clone.1), kind=kCustom, calls=%fused_computation.42 | custom fusion | bytes 1049088 | tf_op jit(solution)/shard_map/scatter | solution.py:104
  65.2 2.1 %convert_bitcast_fusion = bf16[4,8,8192]{2,1,0:T(8,128)(2,1)} fusion(f32[32,8192]{1,0:T(8,128)} %scatter_custom_fusion.2), kind=kLoop, calls=%fused_computation.40 | loop fusion | flops 262144 | bytes 1572864 | tf_op jit(solution)/shard_map/convert_element_type | solution.py:117
  67.3 1.4 all-to-all-done.3
  68.7 4.1 %all-to-all-start.5 = ((bf16[4,8,8192]{2,1,0:T(8,128)(2,1)}), bf16[4,8,8192]{2,1,0:T(8,128)(2,1)}, u32[]{:S(2)}, u32[]{:S(2)}) async-start(bf16[4,8,8192]{2,1,0:T(8,128)(2,1)} %convert_bitcast_fusion), calls=%async_computation.5 | async-start | bytes 1048576 | tf_op jit(solution)/shard_map/all_to_all | solution.py:116
  72.9 0.5 broadcast.183
  73.4 0.7 reduce.9
  74.1 0.1 eq.33
  74.2 1.5 convolution_convert_fusion.1
  75.6 2.3 %convert_element_type.92 = bf16[8,512,128]{2,1,0:T(8,128)(2,1)} reshape(bf16[64,8192]{1,0:T(8,128)(2,1)} %convolution_convert_fusion.1) | data formatting | bytes 2097152 | tf_op jit(solution)/shard_map/convert_element_type | solution.py:136
  78.0 3.8 %all-to-all-done.5 = bf16[4,8,8192]{2,1,0:T(8,128)(2,1)} async-done(((bf16[4,8,8192]{2,1,0:T(8,128)(2,1)}), bf16[4,8,8192]{2,1,0:T(8,128)(2,1)}, u32[]{:S(2)}, u32[]{:S(2)}) %all-to-all-start.5) | async-done | bytes 524320 | tf_op jit(solution)/shard_map/all_to_all | solution.py:116
  81.8 6.3 %all-to-all-start.4 = ((bf16[8,512,128]{2,1,0:T(8,128)(2,1)}), bf16[8,512,128]{2,1,0:T(8,128)(2,1)}, u32[]{:S(2)}, u32[]{:S(2)}) async-start(bf16[8,512,128]{2,1,0:T(8,128)(2,1)} %convert_element_type.92), calls=%async_computation.4 | async-start | bytes 2097152 | tf_op jit(solution)/shard_map/all_to_all | solution.py:135
  88.1 2.4 %convolution_convert_fusion = bf16[64,8192]{1,0:T(8,128)(2,1)} fusion(bf16[4,8,8192]{2,1,0:T(8,128)(2,1)} %all-to-all-done.5, s32[32]{0:T(128)S(1)} %eq.33), kind=kOutput, calls=%fused_computation.8 | convolution fusion | flops 34080768 | bytes 1572992 | tf_op jit(solution)/shard_map/dot_general | solution.py:126
  90.5 2.3 %convert_element_type.97 = bf16[8,512,128]{2,1,0:T(8,128)(2,1)} reshape(bf16[64,8192]{1,0:T(8,128)(2,1)} %convolution_convert_fusion) | data formatting | bytes 2097152 | tf_op jit(solution)/shard_map/convert_element_type | solution.py:139
  92.9 21.0 %all-to-all-done.4 = bf16[8,512,128]{2,1,0:T(8,128)(2,1)} async-done(((bf16[8,512,128]{2,1,0:T(8,128)(2,1)}), bf16[8,512,128]{2,1,0:T(8,128)(2,1)}, u32[]{:S(2)}, u32[]{:S(2)}) %all-to-all-start.4) | async-done | bytes 1048608 | tf_op jit(solution)/shard_map/all_to_all | solution.py:135
  113.8 4.2 %all-to-all-start.6 = ((bf16[8,512,128]{2,1,0:T(8,128)(2,1)}), bf16[8,512,128]{2,1,0:T(8,128)(2,1)}, u32[]{:S(2)}, u32[]{:S(2)}) async-start(bf16[8,512,128]{2,1,0:T(8,128)(2,1)} %convert_element_type.97), calls=%async_computation.6 | async-start | bytes 2097152 | tf_op jit(solution)/shard_map/all_to_all | solution.py:138
  118.1 0.2 reshape.240
  118.3 0.5 fusion.13
  118.8 0.2 copy.38
  119.0 1.0 copy.41
  120.0 2.1 %reduce_sum.57 = bf16[512,128]{1,0:T(8,128)(2,1)} reduce(bf16[8,512,128]{2,1,0:T(8,128)(2,1)} %all-to-all-done.4, bf16[]{:T(256)} %constant.94.clone.1), dimensions={0}, to_apply=%region_7.10 | reduce | flops 458752 | bytes 1179650 | tf_op jit(solution)/shard_map/reduce_sum | solution.py:142
  122.0 21.6 %all-to-all-done.6 = bf16[8,512,128]{2,1,0:T(8,128)(2,1)} async-done(((bf16[8,512,128]{2,1,0:T(8,128)(2,1)}), bf16[8,512,128]{2,1,0:T(8,128)(2,1)}, u32[]{:S(2)}, u32[]{:S(2)}) %all-to-all-start.6) | async-done | bytes 1048608 | tf_op jit(solution)/shard_map/all_to_all | solution.py:138
  143.6 2.1 %reduce_sum.58 = bf16[512,128]{1,0:T(8,128)(2,1)} reduce(bf16[8,512,128]{2,1,0:T(8,128)(2,1)} %all-to-all-done.6, bf16[]{:T(256)} %constant.94.clone.1), dimensions={0}, to_apply=%region_9.12 | reduce | flops 458752 | bytes 1179650 | tf_op jit(solution)/shard_map/reduce_sum | solution.py:143
  (15 shorter events, 0.2 us)
Async XLA Ops:
  0.6 41.1 %copy-start = (bf16[512,2,128]{2,1,0:T(2,128)(2,1)S(1)}, bf16[512,2,128]{2,1,0:T(2,128)(2,1)}, u32[]{:S(2)}) copy-start(bf16[512,2,128]{2,1,0:T(2,128)(2,1)} %param.10) | copy-start | bytes 786436
  4.8 7.9 %all-to-all-start = ((s32[4,1,8]{2,1,0:T(1,128)}), s32[4,1,8]{2,1,0:T(1,128)S(1)}, u32[]{:S(2)}, u32[]{:S(2)}) async-start(s32[4,1,8]{2,1,0:T(1,128)} %bitcast.3), calls=%async_computation | async-start | bytes 4096 | tf_op jit(solution)/shard_map/all_to_all | solution.py:49
  13.7 16.8 %copy-start.2 = (bf16[512,2,128]{2,1,0:T(2,128)(2,1)S(1)}, bf16[512,2,128]{2,1,0:T(2,128)(2,1)}, u32[]{:S(2)}) copy-start(bf16[512,2,128]{2,1,0:T(2,128)(2,1)} %param.13) | copy-start | bytes 786436
  26.8 12.3 %all-to-all-start.2 = ((bf16[4,8,8192]{2,1,0:T(8,128)(2,1)}), bf16[4,8,8192]{2,1,0:T(8,128)(2,1)S(1)}, u32[]{:S(2)}, u32[]{:S(2)}) async-start(bf16[4,8,8192]{2,1,0:T(8,128)(2,1)} %get-tuple-element.15), calls=%async_computation.2 | async-start | bytes 1048576 | tf_op jit(solution)/shard_map/all_to_all | solution.py:53
  44.3 2.3 %copy-start.1 = (bf16[2,1024,128,1]{2,1,0,3:T(8,128)(2,1)S(1)}, bf16[2,1024,128,1]{2,1,0,3:T(8,128)(2,1)}, u32[]{:S(2)}) copy-start(bf16[2,1024,128,1]{2,1,0,3:T(8,128)(2,1)} %reshape.326) | copy-start | bytes 1572868
  56.5 12.3 %all-to-all-start.3 = ((bf16[4,8,8192]{2,1,0:T(8,128)(2,1)}), bf16[4,8,8192]{2,1,0:T(8,128)(2,1)S(1)}, u32[]{:S(2)}, u32[]{:S(2)}) async-start(bf16[4,8,8192]{2,1,0:T(8,128)(2,1)} %convert_bitcast_fusion.1), calls=%async_computation.3 | async-start | bytes 1048576 | tf_op jit(solution)/shard_map/all_to_all | solution.py:113
  68.7 13.1 %all-to-all-start.5 = ((bf16[4,8,8192]{2,1,0:T(8,128)(2,1)}), bf16[4,8,8192]{2,1,0:T(8,128)(2,1)}, u32[]{:S(2)}, u32[]{:S(2)}) async-start(bf16[4,8,8192]{2,1,0:T(8,128)(2,1)} %convert_bitcast_fusion), calls=%async_computation.5 | async-start | bytes 1048576 | tf_op jit(solution)/shard_map/all_to_all | solution.py:116
  81.8 32.0 %all-to-all-start.4 = ((bf16[8,512,128]{2,1,0:T(8,128)(2,1)}), bf16[8,512,128]{2,1,0:T(8,128)(2,1)}, u32[]{:S(2)}, u32[]{:S(2)}) async-start(bf16[8,512,128]{2,1,0:T(8,128)(2,1)} %convert_element_type.92), calls=%async_computation.4 | async-start | bytes 2097152 | tf_op jit(solution)/shard_map/all_to_all | solution.py:135
  113.8 29.8 %all-to-all-start.6 = ((bf16[8,512,128]{2,1,0:T(8,128)(2,1)}), bf16[8,512,128]{2,1,0:T(8,128)(2,1)}, u32[]{:S(2)}, u32[]{:S(2)}) async-start(bf16[8,512,128]{2,1,0:T(8,128)(2,1)} %convert_element_type.97), calls=%async_computation.6 | async-start | bytes 2097152 | tf_op jit(solution)/shard_map/all_to_all | solution.py:138
where the time goes:
time: 147 us; the launch traced here: 146 us
  waiting for transfers between devices  56 us (38%)
  local copies, waits for them, and re-layouts  28.8 us (20%)
  starting transfers between devices  25.8 us (18%)
  other arithmetic  13.1 us (9%)
  blocking collectives  11.3 us (8%)
  matrix products  9.74 us (7%)
    all_to_all x1, waiting for transfers between devices, body(): lax.all_to_all(sent_dv.astype(jnp.bfloat16), 'head', split_axis=0, concat...  21.6 us
    all_to_all x1, waiting for transfers between devices, body(): lax.all_to_all(sent_dk.astype(jnp.bfloat16), 'head', split_axis=0, concat...  21 us
    all_to_all x1, blocking collectives, body(): lax.all_to_all(key_rows, 'ctx', split_axis=0, concat_axis=0, tiled=True)  11.3 us
    all_to_all x1, waiting for transfers between devices, body(): lax.all_to_all(value_rows, 'ctx', split_axis=0, concat_axis=0, tiled=True)  7.53 us
    all_to_all x1, starting transfers between devices, body(): lax.all_to_all(sent_dk.astype(jnp.bfloat16), 'head', split_axis=0, concat...  6.27 us
    all_to_all x1, starting transfers between devices, body(): lax.all_to_all(sent_dv.astype(jnp.bfloat16), 'head', split_axis=0, concat...  4.23 us
    all_to_all x1, starting transfers between devices, body(): lax.all_to_all(requests, 'ctx', split_axis=0, concat_axis=0, tiled=True)  4.21 us
    all_to_all x1, starting transfers between devices, body(): lax.all_to_all(home_dv.astype(jnp.bfloat16), 'ctx', split_axis=0, concat_...  4.14 us
  transfers between devices with their start and end apart: 6, of which 6 were waited for; matrix products, arithmetic and copies ran while one was open for 17% of the time, Pallas kernels for 0%

commit v1 on v0

v1 whole, which is shorter than its diff:
```python
import functools

import jax
import jax.numpy as jnp
from jax import lax
from jax.experimental import pallas as pl
from jax.experimental.pallas import tpu as pltpu
from jax.sharding import PartitionSpec as P

HPG = 16
KBS = 64
TOPB = 16
QBS = 256
CAP = 8
F32 = jnp.float32
BF16 = jnp.bfloat16


def nt(a, b):
    return lax.dot_general(a, b, (((1,), (1,)), ((), ())), preferred_element_type=F32)


def tn(a, b):
    return lax.dot_general(a, b, (((0,), (0,)), ((), ())), preferred_element_type=F32)


def kernel(
    owners, heads, per_group, groups, runs, head_dev, out_blocks,
    req_s, pos_s, inv_s, cnt_s, req_v, kc, vc, q, do,
    dq, dk_out, dv_out,
    ask_v, ask_s, send_k, send_v, got_k, got_v, sel_k, sel_v,
    weights, halves, scores, rowdot, part, yin, zsend, zin, dsend, gath,
    sem_ask, sem_asks, sem_k, sem_v, sem_y, sem_z, sem_d, sem_e, sem_f,
):
    dh = q.shape[1] // head_dev
    keys = TOPB * KBS
    inv_root = dh ** (-0.5)
    c = lax.axis_index("ctx")
    h = lax.axis_index("head")
    my_group = h // per_group
    lo = h % 2
    far = h // 2
    halves_n = heads // 2
    hi_n = per_group // 2
    hi = (h % per_group) // 2
    other = h + 1 - 2 * lo

    def ctx_peer(d):
        return lax.rem(c + d, owners)

    def far_peer(d):
        return lax.rem(far + d, halves_n) * 2 + lo

    def remote(src, dst, sems, i, where):
        return pltpu.make_async_remote_copy(
            src_ref=src, dst_ref=dst, send_sem=sems.at[0, i], recv_sem=sems.at[1, i],
            device_id=where, device_id_type=pl.DeviceIdType.MESH,
        )

    barrier = pltpu.get_barrier_semaphore()
    peers = [(ctx_peer(d), h) for d in range(1, owners)]
    peers += [(c, far_peer(d)) for d in range(1, halves_n)] + [(c, other)]
    for peer in peers:
        pl.semaphore_signal(barrier, inc=1, device_id=peer, device_id_type=pl.DeviceIdType.MESH)
    pl.semaphore_wait(barrier, len(peers))

    ask = {}
    for d in range(1, owners):
        o = ctx_peer(d)
        ask[d] = remote(req_v.at[o], ask_v.at[c], sem_ask, d, (o, h))
        ask[d].start()
    for k in range(CAP):
        at = req_s[c * groups * CAP + my_group * CAP + k]
        got_k[c, k] = kc[at]
        got_v[c, k] = vc[at]

    kv = {}
    for d in range(owners - 1, 0, -1):
        o = lax.rem(c + owners - d, owners)
        ask[d].wait_recv()
        pltpu.make_async_copy(ask_v.at[o], ask_s.at[o], sem_asks.at[d]).start()
    for d in range(owners - 1, 0, -1):
        o = lax.rem(c + owners - d, owners)
        pltpu.make_async_copy(ask_v.at[o], ask_s.at[o], sem_asks.at[d]).wait()
    for cached, sent, got, sems, name in (
        (kc, send_k, got_k, sem_k, 0), (vc, send_v, got_v, sem_v, 1)
    ):
        for d in range(owners - 1, 0, -1):
            o = lax.rem(c + owners - d, owners)
            for k in range(CAP):
                at = ask_s[o, 0, my_group * CAP + k]
                sent[o, k] = cached[at]
            kv[name, d] = remote(sent.at[o], got.at[c], sems, d, (o, h))
            kv[name, d].start()

    def pick(got, sel, name):
        for d in range(1, owners):
            kv[name, d].wait_recv()
        for b in range(runs):
            for t in range(TOPB):
                at = pos_s[b * TOPB + t]
                sel[b, t * KBS : (t + 1) * KBS, :] = got[at // CAP, at % CAP]

    pick(got_k, sel_k, 0)
    tiles = [(b, e) for b in range(runs) for e in range(head_dev)]

    def rows(ref, b, e):
        return ref[b * QBS : (b + 1) * QBS, e * dh : (e + 1) * dh]

    for b, e in tiles:
        live = lax.broadcasted_iota(jnp.int32, (keys, QBS), 0) < cnt_s[b] * KBS
        s = nt(sel_k[b], rows(q, b, e)) * inv_root
        s = jnp.where(live, s, -jnp.inf)
        w = jnp.exp(s - jnp.max(s, axis=0, keepdims=True))
        w = w * (1.0 / jnp.sum(w, axis=0, keepdims=True))
        weights[b, :, e * QBS : (e + 1) * QBS] = w
        halves[b, :, e * QBS : (e + 1) * QBS] = w.astype(BF16)

    pick(got_v, sel_v, 1)

    def stack(ref, b):
        return jnp.concatenate([rows(ref, b, e) for e in range(head_dev)], axis=0)

    def share(x):
        for k in range(CAP):
            for o in range(owners):
                at = inv_s[o * CAP + k]
                part[x, k % 2, k // 2, o] = scores[x, at]
        cp = remote(part.at[x, 1 - lo], yin.at[x], sem_y, x, (c, other))
        cp.start()
        return cp

    def fold(x, cp):
        cp.wait_recv()
        for i in range(hi_n):
            zsend[x, i] = (part[x, lo, i].astype(F32) + yin[x, i].astype(F32)).astype(BF16)
        out = []
        for d in range(1, hi_n):
            to = lax.rem(hi + d, hi_n)
            z = remote(
                zsend.at[x, to], zin.at[x, d], sem_z, x * hi_n + d,
                (c, my_group * per_group + to * 2 + lo),
            )
            z.start()
            out.append(z)
        return out

    def home(x, zs):
        total = zsend[x, hi].astype(F32)
        for d in range(1, hi_n):
            zs[d - 1].wait_recv()
            total = total + zin[x, d].astype(F32)
        dsend[x] = total.astype(BF16)
        gath[x, lo, far, c] = dsend[x, c]
        out = []
        for d in range(1, owners):
            o = ctx_peer(d)
            cp = remote(dsend.at[x, o], gath.at[x, lo, far, c], sem_d, x * owners + d, (o, h))
            cp.start()
            out.append(cp)
        return out

    def spread(x, ds):
        for cp in ds:
            cp.wait_recv()
        out = []
        mine = gath.at[x, lo, far]
        near = [remote(mine, mine, sem_f, x * halves_n, (c, other))]
        for d in range(1, halves_n):
            cp = remote(mine, mine, sem_e, x * halves_n + d, (c, far_peer(d)))
            cp.start()
            out.append(cp)
        near[0].start()
        return out, near

    def relay(x, es, near):
        for d in range(1, halves_n):
            es[d - 1].wait_recv()
            frm = gath.at[x, lo, lax.rem(far + halves_n - d, halves_n)]
            cp = remote(frm, frm, sem_f, x * halves_n + d, (c, other))
            cp.start()
            near.append(cp)
        for cp in near:
            cp.wait_recv()

    scores[:, runs * TOPB] = jnp.zeros((2, KBS, dh), BF16)
    for b in range(runs):
        dv = jnp.dot(halves[b], stack(do, b), preferred_element_type=F32).astype(BF16)
        scores[0, b * TOPB : (b + 1) * TOPB] = dv.reshape(TOPB, KBS, dh)
    y_v = share(0)
    for b, e in tiles:
        cols = slice(e * QBS, (e + 1) * QBS)
        g = rows(do, b, e)
        attn = tn(sel_v[b], halves[b, :, cols]).astype(BF16).astype(F32)
        rd = jnp.sum(g.astype(F32).T * attn, axis=0, keepdims=True)
        ds = (weights[b, :, cols] * (nt(sel_v[b], g) - rd) * inv_root).astype(BF16)
        halves[b, :, cols] = ds
    z_v = fold(0, y_v)
    for b in range(runs):
        dk = jnp.dot(halves[b], stack(q, b), preferred_element_type=F32).astype(BF16)
        scores[1, b * TOPB : (b + 1) * TOPB] = dk.reshape(TOPB, KBS, dh)
    y_k = share(1)
    d_v = home(0, z_v)
    for b, e in tiles:
        part_q = tn(sel_k[b], halves[b, :, e * QBS : (e + 1) * QBS])
        dq[b * QBS : (b + 1) * QBS, e * dh : (e + 1) * dh] = part_q.T.astype(BF16)
    z_k = fold(1, y_k)
    e_v, n_v = spread(0, d_v)
    d_k = home(1, z_k)
    e_k, n_k = spread(1, d_k)
    relay(0, e_v, n_v)

    def collect(x, out):
        for g in range(groups):
            acc = [jnp.zeros((KBS, dh), F32) for _ in range(out_blocks)]
            for src in range(owners):
                for k in range(CAP):
                    own = req_s[c * groups * CAP + g * CAP + k]
                    at = jnp.where(src == c, own, ask_s[src, 0, g * CAP + k]) - h * out_blocks
                    blk = gath[x, k % 2, g * hi_n + k // 2, src].astype(F32)
                    for j in range(out_blocks):
                        acc[j] = acc[j] + blk * jnp.where(at == j, 1.0, 0.0).astype(F32)
            for j in range(out_blocks):
                out[g, j * KBS : (j + 1) * KBS, :] = acc[j].astype(BF16)

    collect(0, dv_out)
    relay(1, e_k, n_k)
    collect(1, dk_out)

    started = list(ask.values()) + list(kv.values()) + [y_v, y_k] + z_v + z_k + d_v + d_k
    for cp in started + e_v + e_k + n_v + n_k:
        cp.wait_send()


def body(queries, cached_keys, cached_values, grad_out, chosen, counts):
    owners = lax.axis_size("ctx")
    heads = lax.axis_size("head")
    qtok, head_dev, dh = queries.shape
    groups, kv_dev, _ = cached_keys.shape
    blk_own = kv_dev // KBS
    runs = qtok // QBS
    per_group = HPG // head_dev
    my_group = lax.axis_index("head") // per_group
    n = runs * TOPB

    live = (jnp.arange(TOPB)[None, None, :] < counts[:, :, None]).reshape(groups, n)
    flat = chosen.reshape(groups, n)
    owner = flat // blk_own
    local = flat % blk_own
    slot = jnp.arange(n)
    same = (owner[:, :, None] == owner[:, None, :]) & live[:, None, :]
    before = same & (slot[None, None, :] < slot[None, :, None])
    rank = jnp.sum(before.astype(jnp.int32), axis=2)
    position = owner * CAP + rank
    spots = jnp.arange(owners * CAP)
    hit = (position[:, None, :] == spots[None, :, None]) & live[:, None, :]
    req = jnp.sum(jnp.where(hit, local[:, None, :], 0), axis=2)
    inv = n + jnp.sum(jnp.where(hit, slot[None, None, :] - n, 0), axis=2)
    req = req.reshape(groups, owners, CAP).transpose(1, 0, 2).reshape(owners, groups * CAP)
    req_v = jnp.pad(req[:, None, :], ((0, 0), (0, 7), (0, 128 - groups * CAP)))
    position = jnp.where(live, position, 0)

    def mine(a):
        return a[0] if groups == 1 else lax.dynamic_index_in_dim(a, my_group, 0, keepdims=False)

    out_blocks = blk_own // heads
    piece = kv_dev // heads
    smem = pl.BlockSpec(memory_space=pltpu.SMEM)
    vmem = pl.BlockSpec(memory_space=pltpu.VMEM)
    keys = TOPB * KBS
    hi_n = per_group // 2
    block = (KBS, dh)
    dma = pltpu.SemaphoreType.DMA
    dq, dk, dv = pl.pallas_call(
        functools.partial(kernel, owners, heads, per_group, groups, runs, head_dev, out_blocks),
        out_shape=(
            jax.ShapeDtypeStruct((qtok, head_dev * dh), BF16),
            jax.ShapeDtypeStruct((groups, piece, dh), BF16),
            jax.ShapeDtypeStruct((groups, piece, dh), BF16),
        ),
        in_specs=[smem] * 4 + [vmem] * 5,
        out_specs=(vmem, vmem, vmem),
        scratch_shapes=[
            pltpu.VMEM((owners, 8, 128), jnp.int32),
            pltpu.SMEM((owners, 8, 128), jnp.int32),
            pltpu.VMEM((owners, CAP) + block, BF16),
            pltpu.VMEM((owners, CAP) + block, BF16),
            pltpu.VMEM((owners, CAP) + block, BF16),
            pltpu.VMEM((owners, CAP) + block, BF16),
            pltpu.VMEM((runs, keys, dh), BF16),
            pltpu.VMEM((runs, keys, dh), BF16),
            pltpu.VMEM((runs, keys, head_dev * QBS), F32),
            pltpu.VMEM((runs, keys, head_dev * QBS), BF16),
            pltpu.VMEM((2, n + 1) + block, BF16),
            pltpu.VMEM((8, QBS), F32),
            pltpu.VMEM((2, 2, CAP // 2, owners) + block, BF16),
            pltpu.VMEM((2, CAP // 2, owners) + block, BF16),
            pltpu.VMEM((2, CAP // 2, owners) + block, BF16),
            pltpu.VMEM((2, hi_n, owners) + block, BF16),
            pltpu.VMEM((2, owners) + block, BF16),
            pltpu.VMEM((2, 2, heads // 2, owners) + block, BF16),
            dma((2, owners)),
            dma((owners,)),
            dma((2, owners)),
            dma((2, owners)),
            dma((2, 2)),
            dma((2, 2 * hi_n)),
            dma((2, 2 * owners)),
            dma((2, heads)),
            dma((2, heads)),
        ],
        compiler_params=pltpu.CompilerParams(
            collective_id=0, has_side_effects=True, vmem_limit_bytes=48 * 1024 * 1024
        ),
    )(
        req.reshape(-1), mine(position), mine(inv), mine(counts), req_v,
        mine(cached_keys).reshape(blk_own, KBS, dh),
        mine(cached_values).reshape(blk_own, KBS, dh),
        queries.reshape(qtok, head_dev * dh),
        grad_out.reshape(qtok, head_dev * dh),
    )
    return dq.reshape(qtok, head_dev, dh), dk, dv


def solution(mesh):
    return jax.shard_map(
        body,
        mesh=mesh,
        in_specs=(
            P("ctx", "head", None),
            P(None, "ctx", None),
            P(None, "ctx", None),
            P("ctx", "head", None),
            P(None, "ctx", None),
            P(None, "ctx"),
        ),
        out_specs=(
            P("ctx", "head", None),
            P(None, ("ctx", "head"), None),
            P(None, ("ctx", "head"), None),
        ),
        check_vma=False,
    )
```

time: 147 us -> 71.2 us (0.48)
  the two profiles are of different devices: /device:TPU:0 before, /device:TPU:12 now
where the time goes in v1:
time: 71.2 us; the launch traced here: 71 us
  Pallas kernels  63.1 us (89%)
  local copies, waits for them, and re-layouts  6.89 us (10%)
    pallas_call x1, Pallas kernels, body(): pl.pallas_call(functools.partial(kernel, owners, heads, per_group, groups...  63.1 us
    unnamed x8, local copies, waits for them, and re-layouts  3.18 us

profile of v1, /device:TPU:12, one launch (start us, length us, event | category | flops | bytes accessed | tf_op | source)
XLA Modules:
  0.0 71.0 jit_solution(11265330329455406577)
XLA Ops:
  0.6 0.0 copy-start
  0.6 0.8 %reshape.498 = s32[32]{0:T(128)S(1)} reshape(s32[1,2,16]{2,1,0:T(2,128)} %param.10) | data formatting | bytes 256 | tf_op jit(solution)/shard_map/reshape | solution.py:247
  1.5 0.7 %lt.57 = s32[2,1,16]{2,0,1:T(2,128)S(1)} broadcast(s32[2]{0:T(128)} %bitcast.14), dimensions={0} | broadcast | bytes 136 | tf_op jit(solution)/shard_map/lt | solution.py:246
  2.2 0.1 lt.58
  2.3 0.1 lt.56
  2.4 0.2 convert_reduce_fusion
  2.6 0.1 select_reduce_fusion
  2.7 0.1 transpose_reshape.3
  2.8 1.1 %copy_bitcast_fusion = (bf16[512,256]{1,0:T(8,128)(2,1)S(1)}, bf16[512,256]{1,0:T(8,128)(2,1)S(1)}) fusion(bf16[64,8,2,128]{3,2,1,0:T(2,128)(2,1)} %bitcast.16, bf16[64,8,2,128]{3,2,1,0:T(2,128)(2,1)} %bitcast.17), kind=kLoop, calls=%fused_computation | loop fusion | bytes 1048576 | tf_op jit(solution)/shard_map/reshape | solution.py:320
  3.9 0.0 copy-start.2
  3.9 0.0 copy-done
  3.9 0.6 copy-done.2
  4.6 0.0 copy-start.1
  4.6 1.2 %copy-done.1 = bf16[1,4096,128]{2,1,0:T(8,128)(2,1)S(1)} copy-done((bf16[1,4096,128]{2,1,0:T(8,128)(2,1)S(1)}, bf16[1,4096,128]{2,1,0:T(8,128)(2,1)}, u32[]{:S(2)}) %copy-start.1) | copy-done | bytes 1048600
  5.8 63.1 %shard_map.88 = (bf16[512,256]{1,0:T(8,128)(2,1)S(1)}, bf16[1,512,128]{2,1,0:T(8,128)(2,1)S(1)}, bf16[1,512,128]{2,1,0:T(8,128)(2,1)S(1)}) custom-call(s32[32]{0:T(128)S(1)} %get-tuple-element.10.req_s, s32[32]{0:T(128)S(1)} %get-tuple-element.11.pos_s, s32[32]{0:T(128)S(1)} %broadcast_add_fusion.inv_s, s32[2]{0:T(128)S(1)} %bitcast.15, ...), custom_call_target="tpu_custom_call" | custom-call | tf_op jit(solution)/shard_map/pallas_call | solution.py:274
  68.9 0.8 %reshape.501 = bf16[512,2,128]{2,1,0:T(2,128)(2,1)} reshape(bf16[512,256]{1,0:T(8,128)(2,1)S(1)} %get-tuple-element.6) | data formatting | bytes 524288 | tf_op jit(solution)/shard_map/reshape | solution.py:322
  69.7 0.7 copy.17
  70.3 0.7 copy.18
  (6 shorter events, 0.0 us)
Async XLA Ops:
  0.6 3.3 %copy-start = (bf16[1,4096,128]{2,1,0:T(8,128)(2,1)S(1)}, bf16[1,4096,128]{2,1,0:T(8,128)(2,1)}, u32[]{:S(2)}) copy-start(bf16[1,4096,128]{2,1,0:T(8,128)(2,1)} %param.7) | copy-start | bytes 3145732
  3.9 0.7 copy-start.2
  4.6 1.2 %copy-start.1 = (bf16[1,4096,128]{2,1,0:T(8,128)(2,1)S(1)}, bf16[1,4096,128]{2,1,0:T(8,128)(2,1)}, u32[]{:S(2)}) copy-start(bf16[1,4096,128]{2,1,0:T(8,128)(2,1)} %param.8) | copy-start | bytes 3145732

commit v2 on v1

v2 whole, which is shorter than its diff:
```python
import functools

import jax
import jax.numpy as jnp
from jax import lax
from jax.experimental import pallas as pl
from jax.experimental.pallas import tpu as pltpu
from jax.sharding import PartitionSpec as P

HPG = 16
KBS = 64
TOPB = 16
QBS = 256
CAP = 8
F32 = jnp.float32
BF16 = jnp.bfloat16


def nt(a, b):
    return lax.dot_general(a, b, (((1,), (1,)), ((), ())), preferred_element_type=F32)


def tn(a, b):
    return lax.dot_general(a, b, (((0,), (0,)), ((), ())), preferred_element_type=F32)


def kernel(
    owners, heads, per_group, groups, runs, head_dev, out_blocks,
    req_s, pos_s, inv_s, cnt_s, req_v, kc_h, vc_h, q_h, do_h,
    dq, dk_out, dv_out,
    kc, vc, q, do,
    ask_v, ask_s, send_k, send_v, got_k, got_v, sel_k, sel_v,
    weights, halves, scores, part, yin, zsend, zin, dsend, gath,
    sem_ask, sem_asks, sem_k, sem_v, sem_y, sem_z, sem_d, sem_e, sem_f, sem_in,
):
    dh = q.shape[1]
    wide = QBS * head_dev
    keys = TOPB * KBS
    inv_root = dh ** (-0.5)
    c = lax.axis_index("ctx")
    h = lax.axis_index("head")
    my_group = h // per_group
    lo = h % 2
    far = h // 2
    halves_n = heads // 2
    hi_n = per_group // 2
    hi = (h % per_group) // 2
    other = h + 1 - 2 * lo

    def ctx_peer(d):
        return lax.rem(c + d, owners)

    def far_peer(d):
        return lax.rem(far + d, halves_n) * 2 + lo

    def remote(src, dst, sems, i, where):
        return pltpu.make_async_remote_copy(
            src_ref=src, dst_ref=dst, send_sem=sems.at[0, i], recv_sem=sems.at[1, i],
            device_id=where, device_id_type=pl.DeviceIdType.MESH,
        )

    pairs = ((kc_h, kc), (q_h, q), (vc_h, vc), (do_h, do))
    loads = [pltpu.make_async_copy(a, b, sem_in.at[i]) for i, (a, b) in enumerate(pairs)]
    for cp in loads:
        cp.start()
    barrier = pltpu.get_barrier_semaphore()
    peers = [(ctx_peer(d), h) for d in range(1, owners)]
    peers += [(c, far_peer(d)) for d in range(1, halves_n)] + [(c, other)]
    for peer in peers:
        pl.semaphore_signal(barrier, inc=1, device_id=peer, device_id_type=pl.DeviceIdType.MESH)
    pl.semaphore_wait(barrier, len(peers))

    ask = {}
    for d in range(1, owners):
        o = ctx_peer(d)
        ask[d] = remote(req_v.at[o], ask_v.at[c], sem_ask, d, (o, h))
        ask[d].start()
    loads[0].wait()
    for k in range(CAP):
        got_k[c, k] = kc[req_s[c, my_group * CAP + k]]

    kv = {}
    for d in range(owners - 1, 0, -1):
        o = lax.rem(c + owners - d, owners)
        ask[d].wait_recv()
        pltpu.make_async_copy(ask_v.at[o], ask_s.at[o], sem_asks.at[d]).start()
    for d in range(owners - 1, 0, -1):
        o = lax.rem(c + owners - d, owners)
        pltpu.make_async_copy(ask_v.at[o], ask_s.at[o], sem_asks.at[d]).wait()
        for k in range(CAP):
            send_k[o, k] = kc[ask_s[o, 0, my_group * CAP + k]]
        kv[0, d] = remote(send_k.at[o], got_k.at[c], sem_k, d, (o, h))
        kv[0, d].start()
    loads[2].wait()
    for d in range(owners - 1, 0, -1):
        o = lax.rem(c + owners - d, owners)
        for k in range(CAP):
            send_v[o, k] = vc[ask_s[o, 0, my_group * CAP + k]]
        kv[1, d] = remote(send_v.at[o], got_v.at[c], sem_v, d, (o, h))
        kv[1, d].start()
    for k in range(CAP):
        got_v[c, k] = vc[req_s[c, my_group * CAP + k]]
    loads[1].wait()
    loads[3].wait()

    def pick(got, sel, name):
        for d in range(1, owners):
            kv[name, d].wait_recv()
        for b in range(runs):
            for t in range(TOPB):
                at = pos_s[b, t]
                sel[b, t * KBS : (t + 1) * KBS, :] = got[at // CAP, at % CAP]

    pick(got_k, sel_k, 0)
    tiles = [(b, e) for b in range(runs) for e in range(head_dev)]

    def rows(ref, b, e):
        at = b * wide + e * QBS
        return ref[at : at + QBS, :]

    order = list(range(1, owners)) + [0]
    y_cp, z_cp, d_cp, e_cp, f_cp = {}, {}, {}, {}, {}

    def share(x):
        for d in order:
            o = ctx_peer(d)
            for k in range(CAP):
                part[x, k % 2, o, k // 2] = scores[x, inv_s[o, k]]
            y_cp[x, d] = remote(
                part.at[x, 1 - lo, o], yin.at[x, d], sem_y, x * owners + d, (c, other)
            )
            y_cp[x, d].start()

    def fold(x):
        for d in order:
            y_cp[x, d].wait_recv()
            for i in range(hi_n):
                both = part[x, lo, ctx_peer(d), i].astype(F32) + yin[x, d, i].astype(F32)
                zsend[x, d, i] = both.astype(BF16)
            for f in range(1, hi_n):
                to = lax.rem(hi + f, hi_n)
                z_cp[x, d, f] = remote(
                    zsend.at[x, d, to], zin.at[x, d, f], sem_z, (x * owners + d) * hi_n + f,
                    (c, my_group * per_group + to * 2 + lo),
                )
                z_cp[x, d, f].start()

    def home(x):
        for d in order:
            total = zsend[x, d, hi].astype(F32)
            for f in range(1, hi_n):
                z_cp[x, d, f].wait_recv()
                total = total + zin[x, d, f].astype(F32)
            if d == 0:
                gath[x, lo, far, c] = total.astype(BF16)
                continue
            o = ctx_peer(d)
            dsend[x, d] = total.astype(BF16)
            d_cp[x, d] = remote(
                dsend.at[x, d], gath.at[x, lo, far, c], sem_d, x * owners + d, (o, h)
            )
            d_cp[x, d].start()

    def spread(x):
        for d in order:
            if d:
                d_cp[x, d].wait_recv()
            src = lax.rem(c + owners - d, owners)
            mine = gath.at[x, lo, far, src]
            at = (x * owners + d) * halves_n
            for f in range(1, halves_n):
                e_cp[x, d, f] = remote(mine, mine, sem_e, at + f, (c, far_peer(f)))
                e_cp[x, d, f].start()
            f_cp[x, d, 0] = remote(mine, mine, sem_f, at, (c, other))
            f_cp[x, d, 0].start()

    def relay(x):
        for d in order:
            src = lax.rem(c + owners - d, owners)
            for f in range(1, halves_n):
                e_cp[x, d, f].wait_recv()
                frm = gath.at[x, lo, lax.rem(far + halves_n - f, halves_n), src]
                at = (x * owners + d) * halves_n + f
                f_cp[x, d, f] = remote(frm, frm, sem_f, at, (c, other))
                f_cp[x, d, f].start()

    def arrived(x):
        for d in order:
            for f in range(halves_n):
                f_cp[x, d, f].wait_recv()

    for b, e in tiles:
        live = lax.broadcasted_iota(jnp.int32, (keys, QBS), 0) < cnt_s[b] * KBS
        s = nt(sel_k[b], rows(q, b, e)) * inv_root
        s = jnp.where(live, s, -jnp.inf)
        w = jnp.exp(s - jnp.max(s, axis=0, keepdims=True))
        w = w * (1.0 / jnp.sum(w, axis=0, keepdims=True))
        weights[b, :, e * QBS : (e + 1) * QBS] = w
        halves[b, :, e * QBS : (e + 1) * QBS] = w.astype(BF16)
    scores[:, runs * TOPB] = jnp.zeros((2, KBS, dh), BF16)

    def partial(x, other_side):
        for b in range(runs):
            side = other_side[b * wide : (b + 1) * wide, :]
            total = jnp.dot(halves[b], side, preferred_element_type=F32).astype(BF16)
            scores[x, b * TOPB : (b + 1) * TOPB] = total.reshape(TOPB, KBS, dh)

    partial(0, do)
    share(0)
    pick(got_v, sel_v, 1)
    for i, (b, e) in enumerate(tiles):
        cols = slice(e * QBS, (e + 1) * QBS)
        g = rows(do, b, e)
        attn = tn(sel_v[b], halves[b, :, cols]).astype(BF16).astype(F32)
        rd = jnp.sum(g.astype(F32).T * attn, axis=0, keepdims=True)
        ds = (weights[b, :, cols] * (nt(sel_v[b], g) - rd) * inv_root).astype(BF16)
        halves[b, :, cols] = ds
        if i == len(tiles) // 2 - 1:
            fold(0)
    partial(1, q)
    share(1)
    home(0)
    for b, e in tiles:
        part_q = tn(sel_k[b], halves[b, :, e * QBS : (e + 1) * QBS])
        at = b * wide + e * QBS
        dq[at : at + QBS, :] = part_q.T.astype(BF16)
    fold(1)
    spread(0)
    home(1)
    relay(0)
    spread(1)
    arrived(0)

    def collect(x, out):
        for g in range(groups):
            acc = [jnp.zeros((KBS, dh), F32) for _ in range(out_blocks)]
            for src in range(owners):
                for k in range(CAP):
                    own = req_s[c, g * CAP + k]
                    at = jnp.where(src == c, own, ask_s[src, 0, g * CAP + k]) - h * out_blocks
                    blk = gath[x, k % 2, g * hi_n + k // 2, src].astype(F32)
                    for j in range(out_blocks):
                        acc[j] = acc[j] + blk * jnp.where(at == j, 1.0, 0.0).astype(F32)
            for j in range(out_blocks):
                out[g, j * KBS : (j + 1) * KBS, :] = acc[j].astype(BF16)

    collect(0, dv_out)
    relay(1)
    arrived(1)
    collect(1, dk_out)

    for group in (ask, kv, y_cp, z_cp, d_cp, e_cp, f_cp):
        for cp in group.values():
            cp.wait_send()


def body(queries, cached_keys, cached_values, grad_out, chosen, counts):
    owners = lax.axis_size("ctx")
    heads = lax.axis_size("head")
    qtok, head_dev, dh = queries.shape
    groups, kv_dev, _ = cached_keys.shape
    blk_own = kv_dev // KBS
    runs = qtok // QBS
    per_group = HPG // head_dev
    my_group = lax.axis_index("head") // per_group
    n = runs * TOPB

    live = jnp.arange(TOPB)[None, None, :] < counts[:, :, None]
    owner = chosen // blk_own
    local = chosen % blk_own
    slot = jnp.arange(runs)[:, None] * TOPB + jnp.arange(TOPB)[None, :]
    same = (owner[:, :, :, None, None] == owner[:, None, None]) & live[:, None, None]
    before = same & (slot[None, None, None] < slot[None, :, :, None, None])
    rank = jnp.sum(before.astype(jnp.int32), axis=(3, 4))
    position = jnp.where(live, owner * CAP + rank, -1)
    spots = jnp.arange(owners)[:, None] * CAP + jnp.arange(CAP)[None, :]
    hit = position[:, None, None] == spots[None, :, :, None, None]
    req = jnp.sum(jnp.where(hit, local[:, None, None], 0), axis=(3, 4))
    inv = n + jnp.sum(jnp.where(hit, slot[None, None, None] - n, 0), axis=(3, 4))
    req = req.transpose(1, 0, 2).reshape(owners, groups * CAP)
    req_v = jnp.pad(req[:, None, :], ((0, 0), (0, 7), (0, 128 - groups * CAP)))
    position = jnp.maximum(position, 0)

    def mine(a):
        return a[0] if groups == 1 else lax.dynamic_index_in_dim(a, my_group, 0, keepdims=False)

    out_blocks = blk_own // heads
    piece = kv_dev // heads
    smem = pl.BlockSpec(memory_space=pltpu.SMEM)
    vmem = pl.BlockSpec(memory_space=pltpu.VMEM)
    hbm = pl.BlockSpec(memory_space=pl.ANY)
    keys = TOPB * KBS
    hi_n = per_group // 2
    block = (KBS, dh)
    dma = pltpu.SemaphoreType.DMA
    dq, dk, dv = pl.pallas_call(
        functools.partial(kernel, owners, heads, per_group, groups, runs, head_dev, out_blocks),
        out_shape=(
            jax.ShapeDtypeStruct((qtok * head_dev, dh), BF16),
            jax.ShapeDtypeStruct((groups, piece, dh), BF16),
            jax.ShapeDtypeStruct((groups, piece, dh), BF16),
        ),
        in_specs=[smem] * 4 + [vmem] + [hbm] * 4,
        out_specs=(vmem, vmem, vmem),
        scratch_shapes=[
            pltpu.VMEM((blk_own,) + block, BF16),
            pltpu.VMEM((blk_own,) + block, BF16),
            pltpu.VMEM((qtok * head_dev, dh), BF16),
            pltpu.VMEM((qtok * head_dev, dh), BF16),
            pltpu.VMEM((owners, 8, 128), jnp.int32),
            pltpu.SMEM((owners, 8, 128), jnp.int32),
            pltpu.VMEM((owners, CAP) + block, BF16),
            pltpu.VMEM((owners, CAP) + block, BF16),
            pltpu.VMEM((owners, CAP) + block, BF16),
            pltpu.VMEM((owners, CAP) + block, BF16),
            pltpu.VMEM((runs, keys, dh), BF16),
            pltpu.VMEM((runs, keys, dh), BF16),
            pltpu.VMEM((runs, keys, head_dev * QBS), F32),
            pltpu.VMEM((runs, keys, head_dev * QBS), BF16),
            pltpu.VMEM((2, n + 1) + block, BF16),
            pltpu.VMEM((2, 2, owners, CAP // 2) + block, BF16),
            pltpu.VMEM((2, owners, CAP // 2) + block, BF16),
            pltpu.VMEM((2, owners, CAP // 2) + block, BF16),
            pltpu.VMEM((2, owners, hi_n) + block, BF16),
            pltpu.VMEM((2, owners) + block, BF16),
            pltpu.VMEM((2, 2, heads // 2, owners) + block, BF16),
            dma((2, owners)),
            dma((owners,)),
            dma((2, owners)),
            dma((2, owners)),
            dma((2, 2 * owners)),
            dma((2, 2 * owners * hi_n)),
            dma((2, 2 * owners)),
            dma((2, owners * heads)),
            dma((2, owners * heads)),
            dma((4,)),
        ],
        compiler_params=pltpu.CompilerParams(
            collective_id=0, has_side_effects=True, vmem_limit_bytes=60 * 1024 * 1024
        ),
    )(
        req, mine(position), mine(inv), mine(counts), req_v,
        mine(cached_keys).reshape(blk_own, KBS, dh),
        mine(cached_values).reshape(blk_own, KBS, dh),
        queries.reshape(qtok * head_dev, dh),
        grad_out.reshape(qtok * head_dev, dh),
    )
    return dq.reshape(qtok, head_dev, dh), dk, dv


def solution(mesh):
    return jax.shard_map(
        body,
        mesh=mesh,
        in_specs=(
            P("ctx", "head", None),
            P(None, "ctx", None),
            P(None, "ctx", None),
            P("ctx", "head", None),
            P(None, "ctx", None),
            P(None, "ctx"),
        ),
        out_specs=(
            P("ctx", "head", None),
            P(None, ("ctx", "head"), None),
            P(None, ("ctx", "head"), None),
        ),
        check_vma=False,
    )
```

time: 71.2 us -> 64.3 us (0.903)
  the two profiles are of different devices: /device:TPU:12 before, /device:TPU:0 now
where the time goes in v2:
time: 64.3 us; the launch traced here: 64.1 us
  Pallas kernels  56.1 us (87%)
  local copies, waits for them, and re-layouts  5.42 us (8%)
  other arithmetic  1.94 us (3%)
  between operations  0.67 us (1%)
    pallas_call x1, Pallas kernels, body(): pl.pallas_call(functools.partial(kernel, owners, heads, per_group, groups...  56.1 us
    unnamed x13, local copies, waits for them, and re-layouts  4.81 us

profile of v2, /device:TPU:0, one launch (start us, length us, event | category | flops | bytes accessed | tf_op | source)
XLA Modules:
  0.0 64.1 jit_solution(9298256155759656989)
XLA Ops:
  0.6 0.0 copy-start.3
  0.6 0.6 %copy-done.3 = s32[1,2]{1,0:T(1,128)S(1)} copy-done((s32[1,2]{1,0:T(1,128)S(1)}, s32[1,2]{1,0:T(1,128)}, u32[]{:S(2)}) %copy-start.3) | copy-done | bytes 32
  1.3 0.1 iota_compare_fusion
  1.4 0.1 iota_add_fusion
  1.4 0.1 iota_add_fusion.1
  1.5 0.0 copy-start.4
  1.5 0.7 %copy-done.4 = s32[1,2,16]{2,1,0:T(2,128)S(1)} copy-done((s32[1,2,16]{2,1,0:T(2,128)S(1)}, s32[1,2,16]{2,1,0:T(2,128)}, u32[]{:S(2)}) %copy-start.4) | copy-done | bytes 152
  2.2 0.2 convert_reduce_fusion
  2.4 0.7 %maximum_bitcast_fusion = (s32[2,16]{1,0:T(2,128)}, s32[1,2,16]{2,1,0:T(2,128)S(1)}) fusion(s32[2,16]{1,0:T(2,128)S(1)} %convert_reduce_fusion, s32[1,2,16]{2,1,0:T(2,128)S(1)} %get-tuple-element.14, s32[2]{0:T(128)S(1)} %bitcast.30), kind=kLoop, calls=%fused_computation.15 | loop fusion | flops 160 | bytes 520 | tf_op jit(solution)/shard_map/squeeze | solution.py:285
  3.0 0.3 fusion.1
  3.3 0.0 copy-start.2
  3.3 0.6 broadcast_add_fusion.inv_s
  3.9 0.0 copy-done.2
  3.9 0.6 pad.4.req_v
  4.5 56.1 %shard_map.88 = (bf16[1024,128]{1,0:T(8,128)(2,1)}, bf16[1,512,128]{2,1,0:T(8,128)(2,1)}, bf16[1,512,128]{2,1,0:T(8,128)(2,1)}) custom-call(s32[4,8]{1,0:T(4,128)} %copy-done.2, s32[2,16]{1,0:T(2,128)} %get-tuple-element.11.pos_s, s32[4,8]{1,0:T(4,128)} %broadcast_add_fusion.inv_s, s32[2]{0:T(128)} %bitcast.28, s32[4,8,128]{2,1,0:T(8,128)} %pad.4.req_v, ...), custom_call_target="tpu_custom_call" | custom-call | tf_op jit(solution)/shard_map/pallas_call | solution.py:296
  60.6 0.0 copy-start.1
  60.6 1.9 %copy.14 = bf16[512,2,128]{2,1,0:T(2,128)(2,1)} copy(bf16[512,2,128]{2,1,0:T(2,128)(2,1)} %bitcast.22) | data formatting | bytes 524288
  62.5 0.0 copy-done.1
  62.5 0.0 copy-start
  62.5 0.7 %copy.15 = bf16[1,512,128]{2,1,0:T(8,128)(2,1)} copy(bf16[1,512,128]{2,1,0:T(8,128)(2,1)S(1)} %copy-done.1) | data formatting | bytes 262144
  63.2 0.3 copy-done
  63.4 0.7 %copy.16 = bf16[1,512,128]{2,1,0:T(8,128)(2,1)} copy(bf16[1,512,128]{2,1,0:T(8,128)(2,1)S(1)} %copy-done) | data formatting | bytes 262144
  (3 shorter events, 0.0 us)
Async XLA Ops:
  0.6 0.7 %copy-start.3 = (s32[1,2]{1,0:T(1,128)S(1)}, s32[1,2]{1,0:T(1,128)}, u32[]{:S(2)}) copy-start(s32[1,2]{1,0:T(1,128)} %param.11) | copy-start | bytes 28
  1.5 0.7 %copy-start.4 = (s32[1,2,16]{2,1,0:T(2,128)S(1)}, s32[1,2,16]{2,1,0:T(2,128)}, u32[]{:S(2)}) copy-start(s32[1,2,16]{2,1,0:T(2,128)} %param.10) | copy-start | bytes 388
  3.3 0.6 copy-start.2
  60.6 1.9 %copy-start.1 = (bf16[1,512,128]{2,1,0:T(8,128)(2,1)S(1)}, bf16[1,512,128]{2,1,0:T(8,128)(2,1)}, u32[]{:S(2)}) copy-start(bf16[1,512,128]{2,1,0:T(8,128)(2,1)} %get-tuple-element.21) | copy-start | bytes 393220
  62.5 1.0 %copy-start = (bf16[1,512,128]{2,1,0:T(8,128)(2,1)S(1)}, bf16[1,512,128]{2,1,0:T(8,128)(2,1)}, u32[]{:S(2)}) copy-start(bf16[1,512,128]{2,1,0:T(8,128)(2,1)} %get-tuple-element.22) | copy-start | bytes 393220

commit v3 on v2

--- a/solution.py
+++ b/solution.py
@@ -131,58 +131,54 @@
             )
             y_cp[x, d].start()
 
-    def fold(x):
-        for d in order:
-            y_cp[x, d].wait_recv()
-            for i in range(hi_n):
-                both = part[x, lo, ctx_peer(d), i].astype(F32) + yin[x, d, i].astype(F32)
-                zsend[x, d, i] = both.astype(BF16)
-            for f in range(1, hi_n):
-                to = lax.rem(hi + f, hi_n)
-                z_cp[x, d, f] = remote(
-                    zsend.at[x, d, to], zin.at[x, d, f], sem_z, (x * owners + d) * hi_n + f,
-                    (c, my_group * per_group + to * 2 + lo),
-                )
-                z_cp[x, d, f].start()
-
-    def home(x):
-        for d in order:
-            total = zsend[x, d, hi].astype(F32)
-            for f in range(1, hi_n):
-                z_cp[x, d, f].wait_recv()
-                total = total + zin[x, d, f].astype(F32)
-            if d == 0:
-                gath[x, lo, far, c] = total.astype(BF16)
-                continue
-            o = ctx_peer(d)
-            dsend[x, d] = total.astype(BF16)
-            d_cp[x, d] = remote(
-                dsend.at[x, d], gath.at[x, lo, far, c], sem_d, x * owners + d, (o, h)
+    def fold(x, d):
+        y_cp[x, d].wait_recv()
+        for i in range(hi_n):
+            both = part[x, lo, ctx_peer(d), i].astype(F32) + yin[x, d, i].astype(F32)
+            zsend[x, d, i] = both.astype(BF16)
+        for f in range(1, hi_n):
+            to = lax.rem(hi + f, hi_n)
+            z_cp[x, d, f] = remote(
+                zsend.at[x, d, to], zin.at[x, d, f], sem_z, (x * owners + d) * hi_n + f,
+                (c, my_group * per_group + to * 2 + lo),
             )
-            d_cp[x, d].start()
-
-    def spread(x):
-        for d in order:
-            if d:
-                d_cp[x, d].wait_recv()
-            src = lax.rem(c + owners - d, owners)
-            mine = gath.at[x, lo, far, src]
-            at = (x * owners + d) * halves_n
-            for f in range(1, halves_n):
-                e_cp[x, d, f] = remote(mine, mine, sem_e, at + f, (c, far_peer(f)))
-                e_cp[x, d, f].start()
-            f_cp[x, d, 0] = remote(mine, mine, sem_f, at, (c, other))
-            f_cp[x, d, 0].start()
-
-    def relay(x):
-        for d in order:
-            src = lax.rem(c + owners - d, owners)
-            for f in range(1, halves_n):
-                e_cp[x, d, f].wait_recv()
-                frm = gath.at[x, lo, lax.rem(far + halves_n - f, halves_n), src]
-                at = (x * owners + d) * halves_n + f
-                f_cp[x, d, f] = remote(frm, frm, sem_f, at, (c, other))
-                f_cp[x, d, f].start()
+            z_cp[x, d, f].start()
+
+    def home(x, d):
+        total = zsend[x, d, hi].astype(F32)
+        for f in range(1, hi_n):
+            z_cp[x, d, f].wait_recv()
+            total = total + zin[x, d, f].astype(F32)
+        if d == 0:
+            gath[x, lo, far, c] = total.astype(BF16)
+            return
+        o = ctx_peer(d)
+        dsend[x, d] = total.astype(BF16)
+        d_cp[x, d] = remote(
+            dsend.at[x, d], gath.at[x, lo, far, c], sem_d, x * owners + d, (o, h)
+        )
+        d_cp[x, d].start()
+
+    def spread(x, d):
+        if d:
+            d_cp[x, d].wait_recv()
+        src = lax.rem(c + owners - d, owners)
+        mine = gath.at[x, lo, far, src]
+        at = (x * owners + d) * halves_n
+        for f in range(1, halves_n):
+            e_cp[x, d, f] = remote(mine, mine, sem_e, at + f, (c, far_peer(f)))
+            e_cp[x, d, f].start()
+        f_cp[x, d, 0] = remote(mine, mine, sem_f, at, (c, other))
+        f_cp[x, d, 0].start()
+
+    def relay(x, d):
+        src = lax.rem(c + owners - d, owners)
+        for f in range(1, halves_n):
+            e_cp[x, d, f].wait_recv()
+            frm = gath.at[x, lo, lax.rem(far + halves_n - f, halves_n), src]
+            at = (x * owners + d) * halves_n + f
+            f_cp[x, d, f] = remote(frm, frm, sem_f, at, (c, other))
+            f_cp[x, d, f].start()
 
     def arrived(x):
         for d in order:
@@ -215,37 +211,44 @@
         rd = jnp.sum(g.astype(F32).T * attn, axis=0, keepdims=True)
         ds = (weights[b, :, cols] * (nt(sel_v[b], g) - rd) * inv_root).astype(BF16)
         halves[b, :, cols] = ds
-        if i == len(tiles) // 2 - 1:
-            fold(0)
+        for d in order[owners * i // len(tiles) : owners * (i + 1) // len(tiles)]:
+            fold(0, d)
     partial(1, q)
     share(1)
-    home(0)
+    for d in order:
+        home(0, d)
     for b, e in tiles:
         part_q = tn(sel_k[b], halves[b, :, e * QBS : (e + 1) * QBS])
         at = b * wide + e * QBS
-        dq[at : at + QBS, :] = part_q.T.astype(BF16)
-    fold(1)
-    spread(0)
-    home(1)
-    relay(0)
-    spread(1)
-    arrived(0)
+        dq[at : at + QBS, :] = part_q.T
+    for d in order:
+        spread(0, d)
+        fold(1, d)
+    for d in order:
+        home(1, d)
+        relay(0, d)
+    for d in order:
+        spread(1, d)
 
     def collect(x, out):
         for g in range(groups):
-            acc = [jnp.zeros((KBS, dh), F32) for _ in range(out_blocks)]
-            for src in range(owners):
-                for k in range(CAP):
-                    own = req_s[c, g * CAP + k]
-                    at = jnp.where(src == c, own, ask_s[src, 0, g * CAP + k]) - h * out_blocks
-                    blk = gath[x, k % 2, g * hi_n + k // 2, src].astype(F32)
-                    for j in range(out_blocks):
-                        acc[j] = acc[j] + blk * jnp.where(at == j, 1.0, 0.0).astype(F32)
-            for j in range(out_blocks):
-                out[g, j * KBS : (j + 1) * KBS, :] = acc[j].astype(BF16)
-
+            for first in range(0, out_blocks, 4):
+                some = range(first, min(first + 4, out_blocks))
+                acc = [jnp.zeros((KBS, dh), F32) for _ in some]
+                for src in range(owners):
+                    for k in range(CAP):
+                        own = req_s[c, g * CAP + k]
+                        at = jnp.where(src == c, own, ask_s[src, 0, g * CAP + k]) - h * out_blocks
+                        blk = gath[x, k % 2, g * hi_n + k // 2, src].astype(F32)
+                        for i, j in enumerate(some):
+                            acc[i] = acc[i] + blk * jnp.where(at == j, 1.0, 0.0).astype(F32)
+                for i, j in enumerate(some):
+                    out[g, j * KBS : (j + 1) * KBS, :] = acc[i]
+
+    arrived(0)
     collect(0, dv_out)
-    relay(1)
+    for d in order:
+        relay(1, d)
     arrived(1)
     collect(1, dk_out)
 
@@ -296,9 +299,9 @@
     dq, dk, dv = pl.pallas_call(
         functools.partial(kernel, owners, heads, per_group, groups, runs, head_dev, out_blocks),
         out_shape=(
-            jax.ShapeDtypeStruct((qtok * head_dev, dh), BF16),
-            jax.ShapeDtypeStruct((groups, piece, dh), BF16),
-            jax.ShapeDtypeStruct((groups, piece, dh), BF16),
+            jax.ShapeDtypeStruct((qtok * head_dev, dh), F32),
+            jax.ShapeDtypeStruct((groups, piece, dh), F32),
+            jax.ShapeDtypeStruct((groups, piece, dh), F32),
         ),
         in_specs=[smem] * 4 + [vmem] + [hbm] * 4,
         out_specs=(vmem, vmem, vmem),
@@ -345,7 +348,7 @@
         queries.reshape(qtok * head_dev, dh),
         grad_out.reshape(qtok * head_dev, dh),
     )
-    return dq.reshape(qtok, head_dev, dh), dk, dv
+    return dq.astype(BF16).reshape(qtok, head_dev, dh), dk.astype(BF16), dv.astype(BF16)
 
 
 def solution(mesh):

time: 64.3 us -> 65.7 us (1.022)
  local copies, waits for them, and re-layouts: 5.42 us -> 2.27 us
  other arithmetic: 1.94 us -> 5.08 us
  Pallas kernels: 56.1 us -> 57.4 us
    convert_element_type x0 -> x3, other arithmetic: none -> 3.15 us  [the longest x1 1.81 us: body(): dq.astype(BF16).reshape(qtok, head_dev, dh)]
    unnamed x13 -> x10, local copies, waits for them, and re-layouts: 4.81 us -> 1.66 us
    pallas_call x1, Pallas kernels: 56.1 us -> 57.4 us  [body(): pl.pallas_call(functools.partial(kernel, owners, heads, per_group, groups...]
where the time goes in v3:
time: 65.7 us; the launch traced here: 65.4 us
  Pallas kernels  57.4 us (87%)
  other arithmetic  5.08 us (8%)
  local copies, waits for them, and re-layouts  2.27 us (3%)
  between operations  0.67 us (1%)
    pallas_call x1, Pallas kernels, body(): pl.pallas_call(functools.partial(kernel, owners, heads, per_group, groups...  57.4 us
    convert_element_type x1, other arithmetic, body(): dq.astype(BF16).reshape(qtok, head_dev, dh)  1.81 us
    unnamed x10, local copies, waits for them, and re-layouts  1.66 us

profile of v3, /device:TPU:0, one launch (start us, length us, event | category | flops | bytes accessed | tf_op | source)
XLA Modules:
  0.0 65.4 jit_solution(26820734941738221)
XLA Ops:
  0.6 0.0 copy-start.3
  0.6 0.6 copy-done.3
  1.3 0.1 iota_compare_fusion
  1.4 0.1 iota_add_fusion
  1.4 0.1 iota_add_fusion.1
  1.5 0.0 copy-start.4
  1.5 0.7 %copy-done.4 = s32[1,2,16]{2,1,0:T(2,128)S(1)} copy-done((s32[1,2,16]{2,1,0:T(2,128)S(1)}, s32[1,2,16]{2,1,0:T(2,128)}, u32[]{:S(2)}) %copy-start.4) | copy-done | bytes 152
  2.2 0.2 convert_reduce_fusion
  2.4 0.6 maximum_bitcast_fusion
  3.0 0.3 fusion.1
  3.3 0.0 copy-start.2
  3.3 0.6 broadcast_add_fusion.inv_s
  3.9 0.0 copy-done.2
  3.9 0.6 pad.4.req_v
  4.5 57.4 %shard_map.88 = (f32[1024,128]{1,0:T(8,128)}, f32[1,512,128]{2,1,0:T(8,128)}, f32[1,512,128]{2,1,0:T(8,128)}) custom-call(s32[4,8]{1,0:T(4,128)} %copy-done.2, s32[2,16]{1,0:T(2,128)} %get-tuple-element.11.pos_s, s32[4,8]{1,0:T(4,128)} %broadcast_add_fusion.inv_s, s32[2]{0:T(128)} %bitcast.28, s32[4,8,128]{2,1,0:T(8,128)} %pad.4.req_v, ...), custom_call_target="tpu_custom_call" | custom-call | tf_op jit(solution)/shard_map/pallas_call | solution.py:299
  61.9 0.0 copy-start.1
  61.9 1.8 %convert_element_type.21 = bf16[1024,128]{1,0:T(8,128)(2,1)} convert(f32[1024,128]{1,0:T(8,128)} %get-tuple-element.6) | non-fusion elementwise | flops 131072 | bytes 786432 | tf_op jit(solution)/shard_map/convert_element_type | solution.py:351
  63.7 0.0 copy-start
  63.7 0.0 copy-done.1
  63.7 0.7 %convert_element_type.22 = bf16[1,512,128]{2,1,0:T(8,128)(2,1)} convert(f32[1,512,128]{2,1,0:T(8,128)S(1)} %copy-done.1) | non-fusion elementwise | flops 65536 | bytes 393216 | tf_op jit(solution)/shard_map/convert_element_type | solution.py:351
  64.4 0.3 copy-done
  64.7 0.7 %convert_element_type.23 = bf16[1,512,128]{2,1,0:T(8,128)(2,1)} convert(f32[1,512,128]{2,1,0:T(8,128)S(1)} %copy-done) | non-fusion elementwise | flops 65536 | bytes 393216 | tf_op jit(solution)/shard_map/convert_element_type | solution.py:351
  (3 shorter events, 0.0 us)
Async XLA Ops:
  0.6 0.7 %copy-start.3 = (s32[1,2]{1,0:T(1,128)S(1)}, s32[1,2]{1,0:T(1,128)}, u32[]{:S(2)}) copy-start(s32[1,2]{1,0:T(1,128)} %param.11) | copy-start | bytes 28
  1.5 0.7 %copy-start.4 = (s32[1,2,16]{2,1,0:T(2,128)S(1)}, s32[1,2,16]{2,1,0:T(2,128)}, u32[]{:S(2)}) copy-start(s32[1,2,16]{2,1,0:T(2,128)} %param.10) | copy-start | bytes 388
  3.3 0.6 copy-start.2
  61.9 1.8 %copy-start.1 = (f32[1,512,128]{2,1,0:T(8,128)S(1)}, f32[1,512,128]{2,1,0:T(8,128)}, u32[]{:S(2)}) copy-start(f32[1,512,128]{2,1,0:T(8,128)} %get-tuple-element.7) | copy-start | bytes 786436
  63.7 1.0 %copy-start = (f32[1,512,128]{2,1,0:T(8,128)S(1)}, f32[1,512,128]{2,1,0:T(8,128)}, u32[]{:S(2)}) copy-start(f32[1,512,128]{2,1,0:T(8,128)} %get-tuple-element.8) | copy-start | bytes 786436
